TPU v7x, 256 devices: a whole 4x4x8 slice. The times are simulated.
256 devices in a mesh: row: 16 (over z, core), col: 16 (over y, x).
Axes of the slice: x: 4, y: 4, z: 8, core: 2. Of those that a mesh axis runs over, the one named last changes fastest.
Arguments:
- vectors: float32 [2048, 48, 512], P(('row', 'col')), may hold values from -6 to 6
- factor_one: float32 [2048, 47, 2048], P('row', None, 'col'), may hold values from -0.125 to 0.125
- factor_two: float32 [2048, 46, 2048], P('row', None, 'col'), may hold values from -0.125 to 0.125
- block_inverse: float32 [2, 2048, 2048], P(None, 'row', 'col'), may hold values from -1 to 2, as said below
- lumped_mass: float32 [2048, 48], P(('row', 'col')), may hold values from 0.25 to 9.5
Outputs:
- solved: float32 [2048, 48, 512], P(('row', 'col'))
- rotated: float32 [2048, 48, 512], P(('row', 'col'))
Inputs may be any that keep to these rules, and one draw needn't show every extreme that they name: Each block of block_inverse is lower triangular with diagonal entries between 0.5 and 2.
All inputs are finite; a program needn't handle non-finite values.
Results may differ from a plain program's by a relative error of at most 0.00013.
Values sent between devices are 32-bit elements; how exact they have to be, the bound alone decides.
No kernel may reach another device: no remote copies, remote signals or barrier semaphores. Data moves between devices by JAX's collectives and lax.ppermute only.
A program may use at most 128 MiB of HBM per device.

v0:
```python
import jax
import jax.numpy as jnp
from jax import lax
from jax.sharding import PartitionSpec as P

ORDER = 98304


def spread(block, axis, holder):
    block = jnp.where(lax.axis_index(axis) == holder, block, jnp.zeros_like(block))
    return lax.psum(block, axis)


def spread_rows(panel_rows):
    grid_block = lax.all_gather(panel_rows, "col", axis=0, tiled=True)
    per_column = lax.axis_size("row") // lax.axis_size("col")
    column = lax.axis_index("col")
    gathered = spread(grid_block, "row", column * per_column + 0)
    return gathered


def solve_panel(panel_rows, inverse_tile):
    needed = spread_rows(panel_rows)
    partial_value = jnp.dot(
        inverse_tile, needed, precision=lax.Precision.HIGHEST, preferred_element_type=jnp.float32
    )
    return lax.psum_scatter(partial_value, "col", scatter_dimension=0, tiled=True)


def trailing(lower_tile, solved_cols):
    return lax.psum_scatter(
        jnp.einsum(
            "jtq,qk->jtk",
            lower_tile,
            solved_cols,
            precision=lax.Precision.HIGHEST,
            preferred_element_type=jnp.float32,
        ),
        "col",
        scatter_dimension=0,
        tiled=True,
    )


def body(vectors, factor_one, factor_two, block_inverse, lumped_mass):
    highest = lax.Precision.HIGHEST
    panel_one = solve_panel(vectors[:, 0, :], block_inverse[0])
    one_cols = spread_rows(panel_one)
    remain = vectors[:, 1:, :] - trailing(factor_one, one_cols)
    panel_two = solve_panel(remain[:, 0, :], block_inverse[1])
    two_cols = spread_rows(panel_two)
    remaining = remain[:, 1:, :] - trailing(factor_two, two_cols)
    solved = jnp.concatenate([panel_one[:, None, :], panel_two[:, None, :], remaining], axis=1)
    weighted = solved * lumped_mass[:, :, None]
    local_gram = jnp.einsum(
        "jtk,jtl->kl", weighted, solved, precision=highest, preferred_element_type=jnp.float32
    )
    mass_gram = lax.psum(local_gram, ("row", "col")) / ORDER
    factor = jnp.linalg.cholesky(mass_gram)
    flattened = solved.reshape(-1, solved.shape[2])
    rotated = jax.scipy.linalg.solve_triangular(factor, flattened.T, lower=True).T
    return (solved, rotated.reshape(solved.shape))


def solution(mesh):
    placed = (
        P(("row", "col"), None, None),
        P("row", None, "col"),
        P("row", None, "col"),
        P(None, "row", "col"),
        P(("row", "col"), None),
    )
    return jax.shard_map(
        body,
        mesh=mesh,
        in_specs=placed,
        out_specs=(P(("row", "col"), None, None), P(("row", "col"), None, None)),
        check_vma=False,
    )
```

profile of v0, /device:TPU:2, one launch (start us, length us, event | category | flops | bytes accessed | tf_op | source)
XLA Modules:
  0.0 1415.3 jit_solution(13320057616582228687)
XLA Ops:
  8.3 23.8 %all-gather = f32[128,1,512]{2,1,0:T(1,128)S(1)} all-gather(f32[8,1,512]{2,1,0:T(1,128)S(1)} %slice.132), channel_id=2, replica_groups=mesh['row'=16,'col'=16] {'col'}, dimensions={0}, use_global_device_ids=true | all-gather | bytes 278528 | tf_op jit(solution)/shard_map/all_gather | solution.py:15
  33.1 109.6 %all-reduce.11.cloned.1.call-done = f32[128,512]{1,0:T(8,128)} async-done(((f32[128,512]{1,0:T(8,128)}), f32[128,512]{1,0:T(8,128)}) %all-reduce.11.cloned.1.call-update) | async-done | bytes 262160 | tf_op jit(solution)/shard_map/psum | solution.py:11
  142.6 2.2 convolution_bitcast_fusion.4
  145.0 1.3 dynamic-slice.3
  146.9 94.3 %all-reduce.21.cloned.1.call-done = f32[128,512]{0,1:T(8,128)} async-done(((f32[128,512]{0,1:T(8,128)}), f32[128,512]{0,1:T(8,128)}) %all-reduce.21.cloned.1.call-update) | async-done | bytes 262160
  242.3 24.2 %all_gather.13 = f32[128,512]{1,0:T(8,128)} all-gather(f32[8,512]{1,0:T(8,128)S(1)} %copy.41), channel_id=1, replica_groups=mesh['row'=16,'col'=16] {'col'}, dimensions={0}, use_global_device_ids=true | all-gather | bytes 278528 | tf_op jit(solution)/shard_map/all_gather | solution.py:15
  266.5 1.1 copy.42
  268.4 108.2 %all-reduce.13.cloned.1.call-done = f32[128,512]{0,1:T(8,128)} async-done(((f32[128,512]{0,1:T(8,128)}), f32[128,512]{0,1:T(8,128)}) %all-reduce.13.cloned.1.call-update) | async-done | bytes 262160 | tf_op jit(solution)/shard_map/psum | solution.py:11
  376.6 13.6 convolution_bitcast_fusion
  390.2 12.7 copy.43
  403.0 99.3 %reduce-scatter.5.cloned.1.call-done = f32[8,47,512]{2,1,0:T(8,128)} async-done(((f32[128,47,512]{2,1,0:T(8,128)}), f32[8,47,512]{2,1,0:T(8,128)}) %reduce-scatter.5.cloned.1.call-update) | async-done | bytes 770064 | tf_op jit(solution)/shard_map/reduce_scatter | solution.py:31
  502.3 1.5 slice_subtract_fusion.1
  504.7 22.2 %all-gather.1 = f32[128,1,512]{2,1,0:T(1,128)S(1)} all-gather(f32[8,1,512]{2,1,0:T(1,128)S(1)} %slice.149), channel_id=3, replica_groups=mesh['row'=16,'col'=16] {'col'}, dimensions={0}, use_global_device_ids=true | all-gather | bytes 278528 | tf_op jit(solution)/shard_map/all_gather | solution.py:15
  527.9 108.6 %all-reduce.15.cloned.1.call-done = f32[128,512]{1,0:T(8,128)} async-done(((f32[128,512]{1,0:T(8,128)}), f32[128,512]{1,0:T(8,128)}) %all-reduce.15.cloned.1.call-update) | async-done | bytes 262160 | tf_op jit(solution)/shard_map/psum | solution.py:11
  636.6 2.2 convolution_bitcast_fusion.3
  638.9 95.7 %all-reduce.23.cloned.1.call-done = f32[128,512]{0,1:T(8,128)} async-done(((f32[128,512]{0,1:T(8,128)}), f32[128,512]{0,1:T(8,128)}) %all-reduce.23.cloned.1.call-update) | async-done | bytes 262160
  735.7 24.2 %all_gather.15 = f32[128,512]{1,0:T(8,128)} all-gather(f32[8,512]{1,0:T(8,128)S(1)} %copy.45), channel_id=1, replica_groups=mesh['row'=16,'col'=16] {'col'}, dimensions={0}, use_global_device_ids=true | all-gather | bytes 278528 | tf_op jit(solution)/shard_map/all_gather | solution.py:15
  759.9 1.1 copy.46
  762.0 108.0 %all-reduce.17.cloned.1.call-done = f32[128,512]{0,1:T(8,128)} async-done(((f32[128,512]{0,1:T(8,128)}), f32[128,512]{0,1:T(8,128)}) %all-reduce.17.cloned.1.call-update) | async-done | bytes 262160 | tf_op jit(solution)/shard_map/psum | solution.py:11
  870.0 13.5 convolution_bitcast_fusion.1
  883.5 12.6 copy.47
  897.5 98.2 %reduce-scatter.7.cloned.1.call-done = f32[8,46,512]{2,1,0:T(8,128)} async-done(((f32[128,46,512]{2,1,0:T(8,128)}), f32[8,46,512]{2,1,0:T(8,128)}) %reduce-scatter.7.cloned.1.call-update) | async-done | bytes 753680 | tf_op jit(solution)/shard_map/reduce_scatter | solution.py:31
  995.7 1.3 slice_subtract_fusion
  997.2 3.0 convolution_bitcast_fusion.2
  1000.2 1.1 copy.50
  1001.4 255.4 %all-reduce.19.cloned.1.call-done = f32[512,512]{0,1:T(8,128)} async-done(((f32[512,512]{0,1:T(8,128)}), f32[512,512]{0,1:T(8,128)}) %all-reduce.19.cloned.1.call-update) | async-done | bytes 1048592 | tf_op jit(solution)/shard_map/psum | solution.py:58
  1256.8 2.5 broadcast_multiply_fusion
  1259.3 1.6 copy.49
  1262.1 11.7 cholesky.104
  1273.9 9.8 custom-call.31
  1283.8 1.2 constant_dynamic-update-slice_fusion.3
  1285.1 1.3 convolution_subtract_fusion.3
  1286.4 12.1 cholesky.217
  1298.6 9.8 custom-call.32
  1308.6 1.3 convolution_subtract_fusion.4
  1309.9 11.7 cholesky.238
  1322.4 9.8 custom-call.33
  1332.4 1.2 convolution_subtract_fusion.5
  1333.7 11.9 cholesky.255
  1349.6 10.5 while.1
  1350.3 2.0 bitcast_dynamic-update-slice_fusion.2
  1352.9 2.0 bitcast_dynamic-update-slice_fusion.2
  1355.5 2.0 bitcast_dynamic-update-slice_fusion.2
  1358.2 2.0 bitcast_dynamic-update-slice_fusion.2
  1360.1 40.2 %custom-call.34 = f32[4,128,128]{1,2,0:T(8,128)S(1)} custom-call(f32[4,128,128]{2,1,0:T(8,128)} %get-tuple-element.9), custom_call_target="InvertDiagBlocksLowerTriangular" | custom-call | tf_op jit(solution)/shard_map/jit(_solve_triangular)/triangular_solve | solution.py:61
  1401.4 1.6 convolution_subtract_fusion.1
  1403.4 1.6 convolution_subtract_fusion
  1406.3 2.3 copy.51
  (95 shorter events, 19.4 us)
Async XLA Ops:
  7.2 369.4 %copy-start = (f32[128,47,128]{2,0,1:T(8,128)S(1)}, f32[128,47,128]{2,0,1:T(8,128)}, u32[]{:S(2)}) copy-start(f32[128,47,128]{2,0,1:T(8,128)} %param.6) | copy-start | bytes 9240580
  7.2 135.5 %all-reduce.11.cloned.1.call-start = ((), (), s32[]{:S(2)}) async-start(), calls=%async_computation.2 | async-start | bytes 524288 | tf_op jit(solution)/shard_map/psum | solution.py:11
  33.0 208.1 %all-reduce.21.cloned.1.call-start = ((), (), s32[]{:S(2)}) async-start(), calls=%async_computation.9 | async-start | bytes 524288
  144.9 231.7 %all-reduce.13.cloned.1.call-start = ((), (), s32[]{:S(2)}) async-start(), calls=%async_computation.3 | async-start | bytes 524288 | tf_op jit(solution)/shard_map/psum | solution.py:11
  268.3 233.9 %reduce-scatter.5.cloned.1.call-start = ((), (), s32[]{:S(2)}) async-start(), calls=%async_computation.4 | async-start | bytes 13369344 | tf_op jit(solution)/shard_map/reduce_scatter | solution.py:31
  402.9 233.7 %copy-start.12 = (f32[2,128,128]{2,1,0:T(8,128)S(1)}, f32[2,128,128]{2,1,0:T(8,128)}, u32[]{:S(2)}) copy-start(f32[2,128,128]{2,1,0:T(8,128)} %param.8) | copy-start | bytes 393220
  402.9 467.1 %copy-start.3 = (f32[128,46,128]{2,0,1:T(8,128)S(1)}, f32[128,46,128]{2,0,1:T(8,128)}, u32[]{:S(2)}) copy-start(f32[128,46,128]{2,0,1:T(8,128)} %param.7) | copy-start | bytes 9043972
  402.9 233.6 %all-reduce.15.cloned.1.call-start = ((), (), s32[]{:S(2)}) async-start(), calls=%async_computation.5 | async-start | bytes 524288 | tf_op jit(solution)/shard_map/psum | solution.py:11
  503.8 0.9 copy-start.5
  527.9 206.7 %all-reduce.23.cloned.1.call-start = ((), (), s32[]{:S(2)}) async-start(), calls=%async_computation.10 | async-start | bytes 524288
  638.8 231.2 %all-reduce.17.cloned.1.call-start = ((), (), s32[]{:S(2)}) async-start(), calls=%async_computation.6 | async-start | bytes 524288 | tf_op jit(solution)/shard_map/psum | solution.py:11
  761.8 233.9 %reduce-scatter.7.cloned.1.call-start = ((), (), s32[]{:S(2)}) async-start(), calls=%async_computation.7 | async-start | bytes 13369344 | tf_op jit(solution)/shard_map/reduce_scatter | solution.py:31
  896.1 0.9 copy-start.10
  896.1 1.2 copy-start.11
  896.1 99.6 %copy-start.6 = (f32[8,47,512]{2,1,0:T(8,128)S(1)}, f32[8,47,512]{2,1,0:T(8,128)}, u32[]{:S(2)}) copy-start(f32[8,47,512]{2,1,0:T(8,128)} %copy-done.5) | copy-start | bytes 2310148
  896.1 101.0 %copy-start.13 = (f32[8,48]{1,0:T(8,128)S(1)}, f32[8,48]{1,0:T(8,128)}, u32[]{:S(2)}) copy-start(f32[8,48]{1,0:T(8,128)} %param.9) | copy-start | bytes 4612
  896.1 360.7 %all-reduce.19.cloned.1.call-start = ((), (), s32[]{:S(2)}) async-start(), calls=%async_computation.8 | async-start | bytes 2097152 | tf_op jit(solution)/shard_map/psum | solution.py:58
  997.2 262.1 %copy-start.2 = (f32[8,48,512]{2,1,0:T(8,128)}, f32[8,48,512]{2,1,0:T(8,128)S(1)}, u32[]{:S(2)}) copy-start(f32[8,48,512]{2,1,0:T(8,128)S(1)} %pad_maximum_fusion) | copy-start | bytes 2359300
  1256.8 4.0 copy-start.4
  1261.1 1.0 copy-start.9
  1285.0 115.3 %copy-start.7 = (f32[384,512]{0,1:T(8,128)S(1)}, f32[384,512]{0,1:T(8,128)}, u32[]{:S(2)}) copy-start(f32[384,512]{0,1:T(8,128)} %copy.50) | copy-start | bytes 2359300
  1360.1 40.6 %copy-start.8 = (f32[512,512]{1,0:T(8,128)}, f32[512,512]{1,0:T(8,128)S(1)}, u32[]{:S(2)}) copy-start(f32[512,512]{1,0:T(8,128)S(1)} %get-tuple-element.98) | copy-start | bytes 3145732
  1401.0 7.5 copy-start.1
Sparse Core Ops, SparseCore 0:
  33.2 109.4 all-reduce.10
  146.7 94.3 all-reduce.20
  268.5 108.0 all-reduce.12
  403.0 99.2 reduce-scatter.4
  528.0 108.5 all-reduce.14
  640.2 94.3 all-reduce.22
  761.9 108.0 all-reduce.16
  896.2 99.3 reduce-scatter.6
  1001.1 255.6 all-reduce.18
where the time goes:
time: 1420 us
  waiting for transfers between devices  1080 us (76%)
  other arithmetic  128 us (9%)
  blocking collectives  94.3 us (7%)
  local copies, waits for them, and re-layouts  52.5 us (4%)
  matrix products  45.1 us (3%)
  between operations  17.6 us (1%)
    psum x4, waiting for transfers between devices, spread(): return lax.psum(block, axis)  434 us
    psum x1, waiting for transfers between devices, body(): mass_gram = lax.psum(local_gram, ('row', 'col')) / ORDER  255 us
    reduce_scatter x2, waiting for transfers between devices, trailing(): lax.psum_scatter(jnp.einsum('jtq,qk->jtk', lower_tile, solved_cols, preci...  197 us
    unnamed x11, waiting for transfers between devices  190 us
    all_gather x4, blocking collectives, spread_rows(): grid_block = lax.all_gather(panel_rows, 'col', axis=0, tiled=True)  94.3 us
    another operation x14, other arithmetic, body(): factor = jnp.linalg.cholesky(mass_gram)  79 us
    another operation x3, other arithmetic, body(): jax.scipy.linalg.solve_triangular(factor, flattened.T, lower=True)  40.3 us
  transfers between devices with their start and end apart: 9, of which 9 were waited for; matrix products, arithmetic and copies ran while one was open for 0% of the time, Pallas kernels for 0%

commit v1 on v0

--- a/solution.py
+++ b/solution.py
@@ -6,13 +6,31 @@
 ORDER = 98304
 
 
+def ring_gather(value, axis, dim):
+    ways, here, step = (lax.axis_size(axis), lax.axis_index(axis), value.shape[dim])
+    lengths = [n * ways if d == dim else n for d, n in enumerate(value.shape)]
+    full = lax.dynamic_update_slice_in_dim(
+        jnp.zeros(lengths, value.dtype), value, here * step, axis=dim
+    )
+    going_up = going_down = value
+    for far in range(1, ways // 2 + 1):
+        going_up = lax.ppermute(going_up, axis, [(d, (d + 1) % ways) for d in range(ways)])
+        full = lax.dynamic_update_slice_in_dim(full, going_up, (here - far) % ways * step, axis=dim)
+        if 2 * far < ways:
+            going_down = lax.ppermute(going_down, axis, [(d, (d - 1) % ways) for d in range(ways)])
+            full = lax.dynamic_update_slice_in_dim(
+                full, going_down, (here + far) % ways * step, axis=dim
+            )
+    return full
+
+
 def spread(block, axis, holder):
     block = jnp.where(lax.axis_index(axis) == holder, block, jnp.zeros_like(block))
     return lax.psum(block, axis)
 
 
 def spread_rows(panel_rows):
-    grid_block = lax.all_gather(panel_rows, "col", axis=0, tiled=True)
+    grid_block = ring_gather(panel_rows, "col", 0)
     per_column = lax.axis_size("row") // lax.axis_size("col")
     column = lax.axis_index("col")
     gathered = spread(grid_block, "row", column * per_column + 0)

time: 1420 us -> 1730 us (1.22)
  starting transfers between devices: 0.55 us -> 140 us
  waiting for transfers between devices: 1080 us -> 1210 us
  local copies, waits for them, and re-layouts: 52.5 us -> 177 us
  blocking collectives: 94.3 us -> 0 us
    ppermute x0 -> x60, starting transfers between devices: none -> 139 us  [the longest x28 127 us: ring_gather(): lax.ppermute(going_down, axis, [(d, (d - 1) % ways) for d in range(ways)])]
    dynamic_update_slice x0 -> x64, local copies, waits for them, and re-layouts: none -> 122 us  [the longest x32 60.1 us: ring_gather(): lax.dynamic_update_slice_in_dim(full, going_up, (here - far) % ways * ste...]
    ppermute x0 -> x60, waiting for transfers between devices: none -> 115 us  [the longest x32 111 us: ring_gather(): lax.ppermute(going_up, axis, [(d, (d + 1) % ways) for d in range(ways)])]
    all_gather x4 -> x0, blocking collectives: 94.3 us -> none  [spread_rows(): grid_block = lax.all_gather(panel_rows, 'col', axis=0, tiled=True)]
    psum x4, waiting for transfers between devices: 434 us -> 455 us  [spread(): return lax.psum(block, axis)]
  transfers between devices with their start and end apart: 9 -> 69, of which waited for: 9 -> 47; matrix products, arithmetic and copies ran while one was open for 0% -> 7% of each run, Pallas kernels for 0% -> 0%
where the time goes in v1:
time: 1730 us; the launch traced here: 1720 us
  waiting for transfers between devices  1210 us (70%)
  local copies, waits for them, and re-layouts  177 us (10%)
  starting transfers between devices  140 us (8%)
  other arithmetic  129 us (7%)
  matrix products  44.6 us (3%)
  between operations  18.6 us (1%)
    psum x4, waiting for transfers between devices, spread(): return lax.psum(block, axis)  455 us
    psum x1, waiting for transfers between devices, body(): mass_gram = lax.psum(local_gram, ('row', 'col')) / ORDER  255 us
    reduce_scatter x2, waiting for transfers between devices, trailing(): lax.psum_scatter(jnp.einsum('jtq,qk->jtk', lower_tile, solved_cols, preci...  196 us
    unnamed x11, waiting for transfers between devices  191 us
    ppermute x28, starting transfers between devices, ring_gather(): lax.ppermute(going_down, axis, [(d, (d - 1) % ways) for d in range(ways)])  127 us
    ppermute x32, waiting for transfers between devices, ring_gather(): lax.ppermute(going_up, axis, [(d, (d + 1) % ways) for d in range(ways)])  111 us
    another operation x14, other arithmetic, body(): factor = jnp.linalg.cholesky(mass_gram)  78.8 us
    dynamic_update_slice x32, local copies, waits for them, and re-layouts, ring_gather(): lax.dynamic_update_slice_in_dim(full, going_up, (here - far) % ways * ste...  60.1 us
  transfers between devices with their start and end apart: 69, of which 47 were waited for; matrix products, arithmetic and copies ran while one was open for 7% of the time, Pallas kernels for 0%

profile of v1, /device:TPU:2, one launch (start us, length us, event | category | flops | bytes accessed | tf_op | source)
XLA Modules:
  0.0 1721.4 jit_solution(7916802026519151586)
XLA Ops:
  10.9 5.7 collective-permute-done
  25.6 5.3 collective-permute-start.5
  35.3 5.3 collective-permute-start.7
  45.0 5.5 collective-permute-start.9
  55.8 5.6 collective-permute-start.11
  61.4 5.8 collective-permute-done.10
  67.9 5.7 collective-permute-start.13
  73.6 6.5 collective-permute-done.12
  118.1 111.7 %all-reduce.11.cloned.1.call-done = f32[128,512]{0,1:T(8,128)} async-done(((f32[128,512]{0,1:T(8,128)}), f32[128,512]{0,1:T(8,128)}) %all-reduce.11.cloned.1.call-update) | async-done | bytes 262160 | tf_op jit(solution)/shard_map/psum | solution.py:29
  233.2 95.1 %all-reduce.21.cloned.1.call-done = f32[128,512]{0,1:T(8,128)} async-done(((f32[128,512]{0,1:T(8,128)}), f32[128,512]{0,1:T(8,128)}) %all-reduce.21.cloned.1.call-update) | async-done | bytes 262160
  345.6 5.7 collective-permute-start.20
  355.3 5.3 collective-permute-start.22
  365.0 5.3 collective-permute-start.24
  375.4 5.6 collective-permute-start.26
  381.0 5.5 collective-permute-done.25
  387.2 5.7 collective-permute-start.28
  392.9 6.4 collective-permute-done.27
  432.2 114.2 %all-reduce.13.cloned.1.call-done = f32[128,512]{0,1:T(8,128)} async-done(((f32[128,512]{0,1:T(8,128)}), f32[128,512]{0,1:T(8,128)}) %all-reduce.13.cloned.1.call-update) | async-done | bytes 262160 | tf_op jit(solution)/shard_map/psum | solution.py:29
  546.4 13.6 convolution_bitcast_fusion
  560.0 12.7 copy.59
  574.0 98.2 %reduce-scatter.5.cloned.1.call-done = f32[8,47,512]{2,1,0:T(8,128)} async-done(((f32[128,47,512]{2,1,0:T(8,128)}), f32[8,47,512]{2,1,0:T(8,128)}) %reduce-scatter.5.cloned.1.call-update) | async-done | bytes 770064 | tf_op jit(solution)/shard_map/reduce_scatter | solution.py:49
  684.2 5.3 collective-permute-start.35
  691.2 5.3 collective-permute-start.37
  698.3 5.3 collective-permute-start.39
  705.3 5.5 collective-permute-start.41
  712.5 5.3 collective-permute-start.43
  745.9 114.6 %all-reduce.15.cloned.1.call-done = f32[128,512]{0,1:T(8,128)} async-done(((f32[128,512]{0,1:T(8,128)}), f32[128,512]{0,1:T(8,128)}) %all-reduce.15.cloned.1.call-update) | async-done | bytes 262160 | tf_op jit(solution)/shard_map/psum | solution.py:29
  862.5 95.9 %all-reduce.23.cloned.1.call-done = f32[128,512]{0,1:T(8,128)} async-done(((f32[128,512]{0,1:T(8,128)}), f32[128,512]{0,1:T(8,128)}) %all-reduce.23.cloned.1.call-update) | async-done | bytes 262160
  984.8 5.4 collective-permute-start.52
  994.5 5.4 collective-permute-start.54
  1004.9 5.7 collective-permute-start.56
  1010.6 6.1 collective-permute-done.55
  1017.3 5.7 collective-permute-start.58
  1023.0 6.3 collective-permute-done.57
  1062.0 114.8 %all-reduce.17.cloned.1.call-done = f32[128,512]{0,1:T(8,128)} async-done(((f32[128,512]{0,1:T(8,128)}), f32[128,512]{0,1:T(8,128)}) %all-reduce.17.cloned.1.call-update) | async-done | bytes 262160 | tf_op jit(solution)/shard_map/psum | solution.py:29
  1176.8 13.5 convolution_bitcast_fusion.1
  1190.3 12.6 copy.78
  1203.9 98.3 %reduce-scatter.7.cloned.1.call-done = f32[8,46,512]{2,1,0:T(8,128)} async-done(((f32[128,46,512]{2,1,0:T(8,128)}), f32[8,46,512]{2,1,0:T(8,128)}) %reduce-scatter.7.cloned.1.call-update) | async-done | bytes 753680 | tf_op jit(solution)/shard_map/reduce_scatter | solution.py:49
  1308.3 255.2 %all-reduce.19.cloned.1.call-done = f32[512,512]{0,1:T(8,128)} async-done(((f32[512,512]{0,1:T(8,128)}), f32[512,512]{0,1:T(8,128)}) %all-reduce.19.cloned.1.call-update) | async-done | bytes 1048592 | tf_op jit(solution)/shard_map/psum | solution.py:76
  1568.7 11.7 cholesky.104
  1580.6 9.8 custom-call.31
  1592.9 11.9 cholesky.217
  1604.8 9.8 custom-call.32
  1616.2 11.7 cholesky.238
  1628.6 9.8 custom-call.33
  1639.9 11.9 cholesky.255
  1655.8 10.4 while.1
  1666.2 40.2 %custom-call.34 = f32[4,128,128]{1,2,0:T(8,128)S(1)} custom-call(f32[4,128,128]{2,1,0:T(8,128)} %get-tuple-element.9), custom_call_target="InvertDiagBlocksLowerTriangular" | custom-call | tf_op jit(solution)/shard_map/jit(_solve_triangular)/triangular_solve | solution.py:79
  (353 shorter events, 289.2 us)
Async XLA Ops:
  7.2 222.7 %all-reduce.11.cloned.1.call-start = ((), (), s32[]{:S(2)}) async-start(), calls=%async_computation.2 | async-start | bytes 524288 | tf_op jit(solution)/shard_map/psum | solution.py:29
  8.4 8.1 collective-permute-start
  16.6 8.4 collective-permute-start.2
  24.9 9.7 collective-permute-start.4
  25.6 9.2 collective-permute-start.5
  34.6 9.7 collective-permute-start.6
  35.3 9.4 collective-permute-start.7
  44.3 10.8 collective-permute-start.8
  45.0 10.6 collective-permute-start.9
  55.1 12.1 collective-permute-start.10
  55.8 11.7 collective-permute-start.11
  67.2 12.9 collective-permute-start.12
  67.9 44.8 %collective-permute-start.13 = (f32[8,512]{0,1:T(8,128)}, f32[8,512]{0,1:T(8,128)}, u32[]{:S(2)}, u32[]{:S(2)}) collective-permute-start(f32[8,512]{0,1:T(8,128)} %collective-permute-done.11), channel_id=1, source_target_pairs={{0,15},{1,0},{2,1},{3,2},{4,3},{5,4},{6,5},{7,6},{8,7},{9,8},{10,9... | collective-permute-start | bytes 49160 | tf_op jit(solution)/shard_map/ppermute | solution.py:20
  80.1 34.9 %collective-permute-start.14 = (f32[8,512]{0,1:T(8,128)}, f32[8,512]{0,1:T(8,128)}, u32[]{:S(2)}, u32[]{:S(2)}) collective-permute-start(f32[8,512]{0,1:T(8,128)} %collective-permute-done.12), channel_id=1, source_target_pairs={{0,1},{1,2},{2,3},{3,4},{4,5},{5,6},{6,7},{7,8},{8,9},{9,10},{10,1... | collective-permute-start | bytes 49160 | tf_op jit(solution)/shard_map/ppermute | solution.py:17
  118.1 210.3 %all-reduce.21.cloned.1.call-start = ((), (), s32[]{:S(2)}) async-start(), calls=%async_computation.9 | async-start | bytes 524288
  231.9 314.4 %all-reduce.13.cloned.1.call-start = ((), (), s32[]{:S(2)}) async-start(), calls=%async_computation.3 | async-start | bytes 524288 | tf_op jit(solution)/shard_map/psum | solution.py:29
  335.9 9.0 collective-permute-start.17
  344.9 9.7 collective-permute-start.19
  345.6 9.6 collective-permute-start.20
  354.6 9.7 collective-permute-start.21
  355.3 9.2 collective-permute-start.22
  364.3 10.4 collective-permute-start.23
  365.0 10.2 collective-permute-start.24
  374.7 11.8 collective-permute-start.25
  375.4 11.4 collective-permute-start.26
  386.5 12.8 collective-permute-start.27
  387.2 40.1 %collective-permute-start.28 = (f32[8,512]{0,1:T(8,128)}, f32[8,512]{0,1:T(8,128)}, u32[]{:S(2)}, u32[]{:S(2)}) collective-permute-start(f32[8,512]{0,1:T(8,128)} %collective-permute-done.26), channel_id=1, source_target_pairs={{0,15},{1,0},{2,1},{3,2},{4,3},{5,4},{6,5},{7,6},{8,7},{9,8},{10,9... | collective-permute-start | bytes 49160 | tf_op jit(solution)/shard_map/ppermute | solution.py:20
  399.3 29.9 %collective-permute-start.29 = (f32[8,512]{0,1:T(8,128)}, f32[8,512]{0,1:T(8,128)}, u32[]{:S(2)}, u32[]{:S(2)}) collective-permute-start(f32[8,512]{0,1:T(8,128)} %collective-permute-done.27), channel_id=1, source_target_pairs={{0,1},{1,2},{2,3},{3,4},{4,5},{5,6},{6,7},{7,8},{8,9},{9,10},{10,1... | collective-permute-start | bytes 49160 | tf_op jit(solution)/shard_map/ppermute | solution.py:17
  432.0 240.2 %reduce-scatter.5.cloned.1.call-start = ((), (), s32[]{:S(2)}) async-start(), calls=%async_computation.4 | async-start | bytes 13369344 | tf_op jit(solution)/shard_map/reduce_scatter | solution.py:49
  572.8 287.7 %all-reduce.15.cloned.1.call-start = ((), (), s32[]{:S(2)}) async-start(), calls=%async_computation.5 | async-start | bytes 524288 | tf_op jit(solution)/shard_map/psum | solution.py:29
  712.5 29.4 %collective-permute-start.43 = (f32[8,512]{1,0:T(8,128)S(1)}, f32[8,512]{1,0:T(8,128)S(1)}, u32[]{:S(2)}, u32[]{:S(2)}) collective-permute-start(f32[8,512]{1,0:T(8,128)S(1)} %collective-permute-done.41), channel_id=1, source_target_pairs={{0,15},{1,0},{2,1},{3,2},{4,3},{5,4},{6,5},{7,6},{8,7},{9,8},{10,9... | collective-permute-start | bytes 49160 | tf_op jit(solution)/shard_map/ppermute | solution.py:20
  719.6 23.9 %collective-permute-start.44 = (f32[8,512]{1,0:T(8,128)S(1)}, f32[8,512]{1,0:T(8,128)S(1)}, u32[]{:S(2)}, u32[]{:S(2)}) collective-permute-start(f32[8,512]{1,0:T(8,128)S(1)} %collective-permute-done.42), channel_id=1, source_target_pairs={{0,1},{1,2},{2,3},{3,4},{4,5},{5,6},{6,7},{7,8},{8,9},{9,10},{10,1... | collective-permute-start | bytes 49160 | tf_op jit(solution)/shard_map/ppermute | solution.py:17
  745.8 212.6 %all-reduce.23.cloned.1.call-start = ((), (), s32[]{:S(2)}) async-start(), calls=%async_computation.10 | async-start | bytes 524288
  862.5 314.3 %all-reduce.17.cloned.1.call-start = ((), (), s32[]{:S(2)}) async-start(), calls=%async_computation.6 | async-start | bytes 524288 | tf_op jit(solution)/shard_map/psum | solution.py:29
  965.9 9.1 collective-permute-start.47
  975.1 9.7 collective-permute-start.49
  975.1 9.7 collective-permute-start.50
  984.8 9.7 collective-permute-start.51
  984.8 9.7 collective-permute-start.52
  994.5 10.4 collective-permute-start.53
  994.5 10.4 collective-permute-start.54
  1004.8 11.8 collective-permute-start.55
  1004.9 11.8 collective-permute-start.56
  1016.6 12.6 collective-permute-start.57
  1017.3 39.9 %collective-permute-start.58 = (f32[8,512]{0,1:T(8,128)}, f32[8,512]{0,1:T(8,128)}, u32[]{:S(2)}, u32[]{:S(2)}) collective-permute-start(f32[8,512]{0,1:T(8,128)} %collective-permute-done.56), channel_id=1, source_target_pairs={{0,15},{1,0},{2,1},{3,2},{4,3},{5,4},{6,5},{7,6},{8,7},{9,8},{10,9... | collective-permute-start | bytes 49160 | tf_op jit(solution)/shard_map/ppermute | solution.py:20
  1029.3 30.0 %collective-permute-start.59 = (f32[8,512]{0,1:T(8,128)}, f32[8,512]{0,1:T(8,128)}, u32[]{:S(2)}, u32[]{:S(2)}) collective-permute-start(f32[8,512]{0,1:T(8,128)} %collective-permute-done.57), channel_id=1, source_target_pairs={{0,1},{1,2},{2,3},{3,4},{4,5},{5,6},{6,7},{7,8},{8,9},{9,10},{10,1... | collective-permute-start | bytes 49160 | tf_op jit(solution)/shard_map/ppermute | solution.py:17
  1061.9 240.3 %reduce-scatter.7.cloned.1.call-start = ((), (), s32[]{:S(2)}) async-start(), calls=%async_computation.7 | async-start | bytes 13369344 | tf_op jit(solution)/shard_map/reduce_scatter | solution.py:49
  1202.9 360.6 %all-reduce.19.cloned.1.call-start = ((), (), s32[]{:S(2)}) async-start(), calls=%async_computation.8 | async-start | bytes 2097152 | tf_op jit(solution)/shard_map/psum | solution.py:76
  (66 other events, 2166.1 us)
Sparse Core Ops, SparseCore 0:
  118.2 111.6 all-reduce.10
  233.9 94.3 all-reduce.20
  432.1 114.2 all-reduce.12
  572.9 99.2 reduce-scatter.4
  745.9 114.4 all-reduce.14
  864.0 94.3 all-reduce.22
  1062.1 114.6 all-reduce.16
  1203.0 99.1 reduce-scatter.6
  1307.7 255.7 all-reduce.18
